TPU v7x, 256 devices: a whole 4x4x8 slice. The times are simulated.
256 devices in a mesh: replica: 16 (over x, z_hi, core), fsdp: 16 (over y, z_lo).
Axes of the slice: x: 4, y: 4, z: 8 (z_hi: 2, z_lo: 4; z = z_hi * 4 + z_lo), core: 2. Of those that a mesh axis runs over, the one named last changes fastest.
Arguments:
- local_weights: float32 [16, 384, 28672], P('replica', None, 'fsdp'), may hold values from -6 to 6
- base_weights: float32 [384, 28672], P(None, 'fsdp'), may hold values from -6 to 6
- error_buffer: float32 [16, 384, 28672], P('replica', None, 'fsdp'), may hold values from -3 to 3
- momentum: float32 [384, 28672], P(None, 'fsdp'), may hold values from -3 to 3
- keep_index: int32 [224, 3, 256], P('fsdp'), may hold values from 0 to 3999, as said below
Outputs:
- new_momentum: float32 [384, 28672], P(None, 'fsdp')
- new_error: float32 [16, 384, 28672], P('replica', None, 'fsdp')
- weights: bfloat16 [384, 28672], replicated
Inputs may be any that keep to these rules, and one draw needn't show every extreme that they name: keep_index[j, i] lists 256 distinct positions u * 128 + v with u and v below 32; every block lists position 0 and the position with u = v = 31; the same positions serve all replicas.
All inputs are finite; a program needn't handle non-finite values.
Results may differ from a plain program's by a relative error of at most 0.0065.
Values may be sent and summed in bfloat16 or wider, within the bound.
A program may use at most 192 MiB of HBM per device.

v0:
```python
import jax
import jax.numpy as jnp
from jax import lax
from jax.sharding import PartitionSpec as P

BLOCK = 128


outer_rate = 0.7
outer_momentum = 0.9


def dct_table(length):
    frequency = jnp.arange(length, dtype=jnp.float32)[:, None]
    position = jnp.arange(length, dtype=jnp.float32)[None, :]
    norm_scale = jnp.where(frequency == 0, jnp.sqrt(1.0 / length), jnp.sqrt(2.0 / length))
    return norm_scale * jnp.cos(jnp.pi * (2.0 * position + 1.0) * frequency / (2.0 * length))


def encode(blocks, cosine_table):
    halfway = jnp.einsum("iajb,vb->iajv", blocks, cosine_table, precision=lax.Precision.HIGHEST)
    return jnp.einsum("ua,iajv->iujv", cosine_table, halfway, precision=lax.Precision.HIGHEST)


def decode(blocks, cosine_table):
    halfway = jnp.einsum("iujv,vb->iujb", blocks, cosine_table, precision=lax.Precision.HIGHEST)
    return jnp.einsum("ua,iujb->iajb", cosine_table, halfway, precision=lax.Precision.HIGHEST)


def pack_blocks(coefficients, positions):
    col_blocks, row_blocks, slots = positions.shape
    flat = coefficients.transpose(2, 0, 1, 3).reshape(col_blocks, row_blocks, BLOCK * BLOCK)
    return jnp.take_along_axis(flat, positions, axis=2)


def unpack_blocks(packed, positions):
    col_blocks, row_blocks, slots = positions.shape
    flat = jnp.zeros((col_blocks, row_blocks, BLOCK * BLOCK), packed.dtype)
    column_index = jnp.arange(col_blocks, dtype=jnp.int32)[:, None, None]
    row_index = jnp.arange(row_blocks, dtype=jnp.int32)[None, :, None]
    flat = flat.at[column_index, row_index, positions].set(packed)
    return flat.reshape(col_blocks, row_blocks, BLOCK, BLOCK).transpose(1, 2, 0, 3)


def body(local_weights, base_weights, error_buffer, momentum, keep_index):
    cosine_table = dct_table(BLOCK)
    row_count, column_count = base_weights.shape
    row_blocks = row_count // BLOCK
    col_blocks = column_count // BLOCK
    pseudo_gradient = base_weights - local_weights[0] + error_buffer[0]
    coefficients = encode(
        pseudo_gradient.reshape(row_blocks, BLOCK, col_blocks, BLOCK), cosine_table
    )
    packed = pack_blocks(coefficients, keep_index)
    kept_blocks = unpack_blocks(packed, keep_index)
    new_error = pseudo_gradient - decode(kept_blocks, cosine_table).reshape(row_count, column_count)
    replicas = lax.axis_size("replica")
    mean_blocks = (
        lax.psum(kept_blocks.astype(jnp.bfloat16), "replica").astype(jnp.float32) / replicas
    )
    update = decode(mean_blocks, cosine_table).reshape(row_count, column_count)
    new_momentum = outer_momentum * momentum + update
    shard_weights = (base_weights - outer_rate * (update + outer_momentum * new_momentum)).astype(
        jnp.bfloat16
    )
    weights = lax.all_gather(shard_weights, "fsdp", axis=1, tiled=True)
    return (new_momentum, new_error[None], weights)


def solution(mesh):
    return jax.shard_map(
        body,
        mesh=mesh,
        in_specs=(
            P("replica", None, "fsdp"),
            P(None, "fsdp"),
            P("replica", None, "fsdp"),
            P(None, "fsdp"),
            P("fsdp", None, None),
        ),
        out_specs=(P(None, "fsdp"), P("replica", None, "fsdp"), P()),
        check_vma=False,
    )
```

profile of v0, /device:TPU:1, one launch (start us, length us, event | category | flops | bytes accessed | tf_op | source)
XLA Modules:
  0.0 868.1 jit_solution(16650692158950642069)
XLA Ops:
  7.2 0.8 fusion.20
  8.1 0.9 shift-left_or_fusion
  10.7 3.9 bitcast_add_fusion.2
  14.6 2.1 reshape.50
  17.1 5.4 fusion.6
  22.5 2.6 convolution_bitcast_fusion.2
  25.1 2.2 copy.20
  27.3 2.1 reshape.51
  29.4 99.3 %gather_fusion = f32[10752]{0:T(1024)S(1)} fusion(f32[14,3,16384]{2,0,1:T(8,128)S(1)} %reshape.51, s32[10752]{0:T(1024)S(1)} %reshape.59), kind=kCustom, calls=%fused_computation | custom fusion | bytes 215040 | tf_op jit(solution)/shard_map/jit(take_along_axis)/gather | solution.py:33
  128.8 40.7 %scatter_custom_fusion = f32[688128]{0:T(1024)S(1)} fusion(s32[10752]{0:T(1024)S(1)} %reshape.65, f32[10752]{0:T(1024)S(1)} %reshape.67, f32[]{:T(128)} %constant.15.clone.1), kind=kCustom, calls=%fused_computation.22 | custom fusion | bytes 2752516
  169.5 2.2 reshape.57
  171.7 2.4 reshape.52
  174.1 1.3 bitcast_convert_fusion
  175.5 188.0 %all-reduce.2.cloned.1.call-done = bf16[3,128,14,128]{3,1,2,0:T(8,128)(2,1)} async-done(((bf16[3,128,14,128]{3,1,2,0:T(8,128)(2,1)}), bf16[3,128,14,128]{3,1,2,0:T(8,128)(2,1)}) %all-reduce.2.cloned.1.call-update) | async-done | bytes 1376272 | tf_op jit(solution)/shard_map/psum | solution.py:59
  363.5 4.5 fusion.8
  367.9 4.1 convolution_bitcast_fusion.1
  372.0 3.5 copy.22
  375.5 7.2 fusion.3
  382.7 2.9 fusion.4
  385.7 4.1 convolution_bitcast_fusion
  389.7 3.7 copy.24
  393.4 4.8 fusion
  398.2 445.3 %all-gather.2.cloned.1.call-done = bf16[384,28672]{1,0:T(8,128)(2,1)} async-done(((bf16[384,1792]{1,0:T(8,128)(2,1)}), bf16[384,28672]{1,0:T(8,128)(2,1)}) %all-gather.2.cloned.1.call-update) | async-done | bytes 22020112 | tf_op jit(solution)/shard_map/all_gather | solution.py:66
  843.5 17.8 %copy.46 = bf16[384,28672]{1,0:T(8,128)(2,1)} copy(bf16[384,28672]{1,0:T(8,128)(2,1)} %all-gather.2.cloned.1.call-done) | data formatting | bytes 44040192
  (21 shorter events, 2.3 us)
Async XLA Ops:
  7.2 356.3 %all-reduce.2.cloned.1.call-start = ((), (), s32[]{:S(2)}) async-start(), calls=%async_computation | async-start | bytes 2752512 | tf_op jit(solution)/shard_map/psum | solution.py:59
  14.6 2.5 copy-start
  29.4 99.3 %copy-start.2 = (s32[14,3,256]{2,0,1:T(8,128)S(1)}, s32[14,3,256]{2,0,1:T(8,128)}, u32[]{:S(2)}) copy-start(s32[14,3,256]{2,0,1:T(8,128)} %param.9) | copy-start | bytes 129028
  175.5 668.0 %all-gather.2.cloned.1.call-start = ((), (), s32[]{:S(2)}) async-start(), calls=%async_computation.1 | async-start | bytes 23396352 | tf_op jit(solution)/shard_map/all_gather | solution.py:66
  389.7 3.7 copy-start.1
Sparse Core Ops, SparseCore 0:
  175.6 187.8 all-reduce.1
  382.9 460.5 all-gather.1
where the time goes:
time: 869 us; the launch traced here: 868 us
  waiting for transfers between devices  633 us (73%)
  local copies, waits for them, and re-layouts  176 us (20%)
  matrix products  23.5 us (3%)
  other arithmetic  20.6 us (2%)
  between operations  14.2 us (2%)
    all_gather x1, waiting for transfers between devices, body(): weights = lax.all_gather(shard_weights, 'fsdp', axis=1, tiled=True)  445 us
    psum x1, waiting for transfers between devices, body(): lax.psum(kept_blocks.astype(jnp.bfloat16), 'replica').astype(jnp.float32)  188 us
    gather x2, local copies, waits for them, and re-layouts, pack_blocks(): return jnp.take_along_axis(flat, positions, axis=2)  99.3 us
    unnamed x10, local copies, waits for them, and re-layouts  61 us
  transfers between devices with their start and end apart: 2, of which 2 were waited for; matrix products, arithmetic and copies ran while one was open for 2% of the time, Pallas kernels for 0%

commit v1 on v0

v1 whole, which is shorter than its diff:
```python
import functools

import jax
import jax.numpy as jnp
import ml_dtypes
import numpy as np
from jax import lax
from jax.experimental import pallas as pl
from jax.experimental.pallas import tpu as pltpu
from jax.sharding import PartitionSpec as P

MESH = pl.DeviceIdType.MESH
BLOCK = 128
LOWF = 32
N_REPLICA = 16
F32 = jnp.float32
BF16 = jnp.bfloat16
outer_rate = 0.7
outer_momentum = 0.9

TILES = ((0, 512), (512, 512), (1024, 512), (1536, 256))
STAGES = ((0, 96, 32, 32), (192, 96, 32, 32))


def split(values):
    high = values.astype(ml_dtypes.bfloat16)
    low = (values - high.astype(np.float64)).astype(ml_dtypes.bfloat16)
    return high, low


def tables():
    u = np.arange(LOWF, dtype=np.float64)[:, None]
    a = np.arange(BLOCK, dtype=np.float64)[None, :]
    norm = np.where(u == 0, np.sqrt(1.0 / BLOCK), np.sqrt(2.0 / BLOCK))
    low = norm * np.cos(np.pi * (2 * a + 1) * u / (2 * BLOCK))
    diag = np.kron(np.eye(4), low)
    wide = np.concatenate(split(diag), axis=0)
    turned = np.zeros((BLOCK, BLOCK))
    turned[:, :LOWF] = low.T
    narrow = np.concatenate(split(diag.T) + split(low) + split(turned), axis=0)
    return wide, narrow


def mm(a, b):
    return jnp.dot(a, b, preferred_element_type=F32)


def halves(v):
    high = v.astype(BF16)
    return high, (v - high.astype(F32)).astype(BF16)


def three(a, b):
    return mm(a[0], b[0]) + (mm(a[1], b[0]) + mm(a[0], b[1]))


def kernel(
    local_hbm, base_hbm, err_hbm, mom_hbm, keep_hbm, wide_hbm, narrow_hbm,
    z_ref, e_ref, m_ref,
    local, base, err, mom, keep, wide, narrow,
    mask, kept, rs_send, rs_recv, part, mean,
    load_sem, red_send, red_recv, out_sem, in_sem, pair_sem,
):
    r, f = lax.axis_index("replica"), lax.axis_index("fsdp")
    x, zh, c = r // 4, (r // 2) % 2, r % 2
    y, zl = f // 4, f % 4
    z = zh * 4 + zl
    cols = e_ref.shape[1]
    group = x * 2 + c

    def at(x_, y_, z_, c_):
        return ((x_ * 2 + z_ // 4) * 2 + c_, y_ * 4 + z_ % 4)

    device = {
        "x+": at((x + 1) % 4, y, z, c), "x-": at((x + 3) % 4, y, z, c),
        "y+": at(x, (y + 1) % 4, z, c), "y-": at(x, (y + 3) % 4, z, c),
        "z+": at(x, y, (z + 1) % 8, c), "z-": at(x, y, (z + 7) % 8, c),
        "far": at(x, y, (z + 4) % 8, c), "pair": at(x, y, z, 1 - c),
    }
    peers = [(group + k) % 8 for k in range(1, 8)]
    peer_device = [at(p // 2, y, z, p % 2) for p in peers]

    def load(src, dst, n):
        copy = pltpu.make_async_copy(src, dst, load_sem.at[n])
        copy.start()
        return copy

    loads = {"keep": load(keep_hbm, keep, 0), "narrow": load(narrow_hbm, narrow, 1)}
    for i in range(3):
        rows = pl.ds(BLOCK * i, BLOCK)
        loads["base", i] = load(base_hbm.at[rows], base.at[rows], 2 + i)
        loads["local", i] = load(local_hbm.at[0, rows], local.at[rows], 5 + i)
        loads["err", i] = load(err_hbm.at[0, rows], err.at[rows], 8 + i)
    loads["wide"] = load(wide_hbm, wide, 11)
    loads["mom"] = load(mom_hbm, mom, 12)

    barrier = pltpu.get_barrier_semaphore()
    partners = [device[k] for k in ("y+", "y-", "z+", "z-", "far")] + peer_device
    for d in partners:
        pl.semaphore_signal(barrier, inc=1, device_id=d, device_id_type=MESH)

    loads["keep"].wait()
    for i in range(3):
        for t, (_, width) in enumerate(TILES):
            n = width // BLOCK
            at_u, at_v = [], []
            for b in range(n):
                pos = keep[i, pl.ds(4 * t + b, 1), :]
                u = lax.broadcasted_iota(jnp.int32, (LOWF, 256), 0)
                v = lax.broadcasted_iota(jnp.int32, (4 * LOWF, 256), 0)
                at_u.append(jnp.where(u == pos // BLOCK, 1.0, 0.0).astype(BF16))
                at_v.append(jnp.where(v == pos % BLOCK + LOWF * b, 1.0, 0.0).astype(BF16))
            mask[pl.ds(LOWF * i, LOWF), pl.ds(BLOCK * t, BLOCK)] = lax.dot_general(
                jnp.concatenate(at_u, axis=1),
                jnp.concatenate(at_v, axis=1),
                (((1,), (1,)), ((), ())),
                preferred_element_type=F32,
            )

    loads["narrow"].wait()
    low = narrow[1024:1056], narrow[1056:1088]
    turned = narrow[1088:1216, :LOWF], narrow[1216:1344, :LOWF]
    for i in range(3):
        rows = pl.ds(BLOCK * i, BLOCK)
        for name in ("base", "local", "err"):
            loads[name, i].wait()
        for t, (first, width) in enumerate(TILES):
            span = pl.ds(first, width)
            pseudo = base[rows, span] - local[rows, span] + err[rows, span]
            e_ref[rows, span] = pseudo
            diag_t = narrow[0:width], narrow[512 : 512 + width]
            half = three(halves(pseudo), diag_t)
            coef = three(low, halves(half))
            kept[pl.ds(LOWF * i, LOWF), pl.ds(BLOCK * t, BLOCK)] = (
                coef * mask[pl.ds(LOWF * i, LOWF), pl.ds(BLOCK * t, BLOCK)]
            )
    for t in range(4):
        for a in range(2):
            rs_send[4 * a + t] = kept[48 * a : 48 * a + 48, BLOCK * t : BLOCK * t + BLOCK].astype(BF16)

    pl.semaphore_wait(barrier, len(partners))
    scatter = []
    for k in range(7):
        scatter.append(
            pltpu.make_async_remote_copy(
                src_ref=rs_send.at[peers[k]], dst_ref=rs_recv.at[k],
                send_sem=red_send.at[k], recv_sem=red_recv.at[k],
                device_id=peer_device[k], device_id_type=MESH,
            )
        )
        scatter[-1].start()

    loads["wide"].wait()
    diag = wide[0:128], wide[128:256]
    for t, (first, width) in enumerate(TILES):
        spread = three(halves(kept[:, BLOCK * t : BLOCK * t + BLOCK]), (diag[0][:, :width], diag[1][:, :width]))
        for i in range(3):
            back = three(turned, halves(spread[LOWF * i : LOWF * i + LOWF]))
            rows, span = pl.ds(BLOCK * i, BLOCK), pl.ds(first, width)
            e_ref[rows, span] = e_ref[rows, span] - back

    total = rs_send[group].astype(F32)
    for k in range(7):
        scatter[k].wait()
        total = total + rs_recv[k].astype(F32)
    part[0] = total.astype(BF16)
    far = pltpu.make_async_remote_copy(
        src_ref=part.at[0], dst_ref=part.at[1], send_sem=red_send.at[7], recv_sem=red_recv.at[7],
        device_id=device["far"], device_id_type=MESH,
    )
    far.start()
    far.wait()
    mean[group] = ((part[0].astype(F32) + part[1].astype(F32)) * (1.0 / N_REPLICA)).astype(BF16)
    spread_out = []
    for k in range(7):
        spread_out.append(
            pltpu.make_async_remote_copy(
                src_ref=mean.at[group], dst_ref=mean.at[group],
                send_sem=red_send.at[8 + k], recv_sem=red_recv.at[8 + k],
                device_id=peer_device[k], device_id_type=MESH,
            )
        )
        spread_out[-1].start()
    for copy in spread_out:
        copy.wait()

    loads["mom"].wait()
    own = pl.multiple_of(f * cols, BLOCK)
    for t, (first, width) in enumerate(TILES):
        m_t = jnp.concatenate([mean[t], mean[4 + t]], axis=0)
        spread = mm(m_t, diag[0][:, :width]) + mm(m_t, diag[1][:, :width])
        for i in range(3):
            update = three(turned, halves(spread[LOWF * i : LOWF * i + LOWF]))
            rows, span = pl.ds(BLOCK * i, BLOCK), pl.ds(first, width)
            moved = outer_momentum * mom[rows, span] + update
            m_ref[rows, span] = moved
            weights = base[rows, span] - outer_rate * (update + outer_momentum * moved)
            z_ref[rows, pl.ds(pl.multiple_of(own + first, BLOCK), width)] = weights.astype(BF16)

    odd = x % 2

    class Stage:
        def __init__(self, s):
            start, count, outer, middle = STAGES[s]
            first = start + c * count
            self.s, self.count = s, count
            self.size = {"m": middle, "o": outer, "q": outer}
            self.row = {
                "m": first + outer,
                "o": first + odd * (outer + middle),
                "q": first + (1 - odd) * (outer + middle),
            }
            self.names = {}

        def sem(self, key):
            return in_sem.at[self.s, self.names.setdefault(key, len(self.names))]

        def ref(self, p, dy, dz, h):
            column = (((y + dy + 4) % 4) * 4 + (zl + dz + 4) % 4) * cols
            if h is None:
                span = pl.ds(pl.multiple_of(column, BLOCK), cols)
            else:
                span = pl.ds(pl.multiple_of(column + h * (cols // 2), BLOCK), cols // 2)
            return z_ref.at[pl.ds(pl.multiple_of(self.row[p], 16), self.size[p]), span]

        def copy(self, p, a, b, h, way, recv):
            dy, dz = (a, b) if p != "o" else (b, a)
            ref = self.ref(p, dy, dz, h)
            return pltpu.make_async_remote_copy(
                src_ref=ref, dst_ref=ref, send_sem=out_sem.at[self.s, WAYS.index(way)], recv_sem=recv,
                device_id=device[way], device_id_type=MESH,
            )

        def axes(self, p):
            return ("y", "z") if p == "m" else ("z", "y")

        def send(self, p, a, b, h, axis, sign, key):
            way = self.axes(p)[axis] + sign
            self.copy(p, a, b, h, way, self.sem((p,) + key)).start()

        def arrive(self, p, a, b, h, key):
            self.copy(p, a, b, h, "pair", self.sem((p,) + key)).wait_recv()

        def share(self, p, a, b, h):
            self.copy(p, a, b, h, "pair", pair_sem.at[self.s]).start()
            if p == "o":
                for half, way in ((0, "x+"), (1, "x-")):
                    if h is None or h == half:
                        self.copy(p, a, b, half, way, self.sem(("x", a % 4, b % 4, half))).start()

        def begin(self):
            for p in "mo":
                for sign, back in (("+", "-"), ("-", "+")):
                    self.send(p, 0, 0, None, 0, sign, ("A", back, "full"))
            for p in "mo":
                for sign, back in (("+", "-"), ("-", "+")):
                    self.send(p, 0, 0, None, 1, sign, ("B", 0, back, "full"))

        def first_full(self):
            for p in "mo":
                for sign, back, a, h in (("+", "-", -1, 0), ("-", "+", 1, 1)):
                    self.arrive(p, a, 0, None, ("A", back, "full"))
                    self.send(p, a, 0, h, 0, sign, ("A", back, "half"))
                    for sign2, back2 in (("+", "-"), ("-", "+")):
                        self.send(p, a, 0, None, 1, sign2, ("B", a, back2, "full"))
                    self.share(p, a, 0, None)

        def first_half(self):
            for p in "mo":
                for back, h in (("-", 0), ("+", 1)):
                    self.arrive(p, 2, 0, h, ("A", back, "half"))
                    for sign2, back2 in (("+", "-"), ("-", "+")):
                        self.send(p, 2, 0, h, 1, sign2, ("B", 2, back2, h))
                    self.share(p, 2, 0, h)

        def second_full(self, a):
            for p in "mo":
                for sign, back, b, h in (("+", "-", -1, 0), ("-", "+", 1, 1)):
                    self.arrive(p, a, b, None, ("B", a, back, "full"))
                    self.send(p, a, b, h, 1, sign, ("B", a, back, "half"))
                    self.share(p, a, b, None)

        def second_parts(self, h):
            for p in "mo":
                for sign, back, b, forward in (("+", "-", -1, 0), ("-", "+", 1, 1)):
                    self.arrive(p, 2, b, h, ("B", 2, back, h))
                    if h == forward:
                        self.send(p, 2, b, h, 1, sign, ("B", 2, back, "half"))
                    self.share(p, 2, b, h)

        def second_half(self, a):
            for p in "mo":
                for back, h in (("-", 0), ("+", 1)):
                    self.arrive(p, a, 2, h, ("B", a, back, "half"))
                    self.share(p, a, 2, h)

        def across(self, places):
            for a, b in places:
                for h in (0, 1):
                    ref = self.ref("q", b, a, h)
                    copy = functools.partial(
                        pltpu.make_async_remote_copy, src_ref=ref, dst_ref=ref,
                        send_sem=out_sem.at[self.s, WAYS.index("pair")],
                        device_id=device["pair"], device_id_type=MESH,
                    )
                    copy(recv_sem=self.sem(("x", a % 4, b % 4, h))).wait_recv()
                    copy(recv_sem=pair_sem.at[self.s]).start()

        def finish(self):
            outer, middle = self.size["o"], self.size["m"]
            each = 15 * cols // 2

            def drain(way, rows, columns):
                ref = z_ref.at[pl.ds(0, rows), pl.ds(0, columns)]
                pltpu.make_async_remote_copy(
                    src_ref=ref, dst_ref=ref, send_sem=out_sem.at[self.s, WAYS.index(way)],
                    recv_sem=pair_sem.at[self.s], device_id=device["pair"], device_id_type=MESH,
                ).wait_send()

            for way in ("y+", "y-", "z+", "z-"):
                assert outer == middle
                drain(way, outer, each)
            for way in ("x+", "x-"):
                drain(way, outer, each)
            drain("pair", self.count, 15 * cols)
            ref = z_ref.at[pl.ds(0, self.count), pl.ds(0, 15 * cols)]
            pltpu.make_async_remote_copy(
                src_ref=ref, dst_ref=ref, send_sem=out_sem.at[self.s, WAYS.index("pair")],
                recv_sem=pair_sem.at[self.s], device_id=device["pair"], device_id_type=MESH,
            ).wait_recv()

    stages = [Stage(s) for s in range(len(STAGES))]

    def early(g):
        g.first_full()
        g.second_full(0)
        g.first_half()
        g.across([(-1, 0), (1, 0)])
        g.second_full(-1)
        g.second_full(1)
        g.across([(0, -1), (0, 1), (2, 0)])

    def late(g):
        g.second_half(0)
        g.second_parts(0)
        g.second_parts(1)
        g.across([(-1, -1), (-1, 1), (1, -1), (1, 1)])
        g.second_half(-1)
        g.second_half(1)
        g.second_half(2)
        g.across([(0, 2), (2, -1), (2, 1), (-1, 2), (1, 2), (2, 2)])

    stages[0].begin()
    early(stages[0])
    stages[1].begin()
    late(stages[0])
    early(stages[1])
    late(stages[1])
    for g in stages:
        g.finish()


WAYS = ("y+", "y-", "z+", "z-", "x+", "x-", "pair")


def store(z_ref, e_ref, m_ref, w_out, e_out, m_out, sem):
    rows = z_ref.shape[0] // 8
    copies = [
        pltpu.make_async_copy(z_ref.at[pl.ds(rows * k, rows)], w_out.at[pl.ds(rows * k, rows)], sem.at[k])
        for k in range(8)
    ]
    copies.append(pltpu.make_async_copy(e_ref, e_out.at[0], sem.at[8]))
    copies.append(pltpu.make_async_copy(m_ref, m_out, sem.at[9]))
    for copy in copies:
        copy.start()
    for copy in copies:
        copy.wait()


def body(local_weights, base_weights, error_buffer, momentum, keep_index):
    rows, cols = base_weights.shape
    shards = lax.axis_size("fsdp")
    wide, narrow = tables()
    hbm = pl.BlockSpec(memory_space=pltpu.HBM)
    vmem = pl.BlockSpec(memory_space=pltpu.VMEM)
    z, e, m = pl.pallas_call(
        kernel,
        out_shape=(
            pltpu.VMEM((rows, shards * cols), BF16),
            pltpu.VMEM((rows, cols), F32),
            pltpu.VMEM((rows, cols), F32),
        ),
        in_specs=[hbm] * 7,
        out_specs=[vmem] * 3,
        scratch_shapes=[pltpu.VMEM((rows, cols), F32)] * 4
        + [
            pltpu.VMEM((3, 14, 256), jnp.int32),
            pltpu.VMEM((256, 512), BF16),
            pltpu.VMEM((1344, 128), BF16),
            pltpu.VMEM((96, 512), F32),
            pltpu.VMEM((96, 512), F32),
            pltpu.VMEM((8, 48, 128), BF16),
            pltpu.VMEM((7, 48, 128), BF16),
            pltpu.VMEM((2, 48, 128), BF16),
            pltpu.VMEM((8, 48, 128), BF16),
            pltpu.SemaphoreType.DMA((13,)),
            pltpu.SemaphoreType.DMA((15,)),
            pltpu.SemaphoreType.DMA((15,)),
            pltpu.SemaphoreType.DMA((2, 7)),
            pltpu.SemaphoreType.DMA((2, 80)),
            pltpu.SemaphoreType.DMA((2,)),
        ],
        compiler_params=pltpu.CompilerParams(
            collective_id=1, has_side_effects=True, vmem_limit_bytes=30 << 20
        ),
        name="step",
    )(
        local_weights,
        base_weights,
        error_buffer,
        momentum,
        keep_index.transpose(1, 0, 2),
        jnp.asarray(wide),
        jnp.asarray(narrow),
    )
    weights, new_error, new_momentum = pl.pallas_call(
        store,
        out_shape=(
            jax.ShapeDtypeStruct((rows, shards * cols), BF16),
            jax.ShapeDtypeStruct((1, rows, cols), F32),
            jax.ShapeDtypeStruct((rows, cols), F32),
        ),
        in_specs=[vmem] * 3,
        out_specs=[pl.BlockSpec(memory_space=pl.ANY)] * 3,
        scratch_shapes=[pltpu.SemaphoreType.DMA((10,))],
        compiler_params=pltpu.CompilerParams(vmem_limit_bytes=1 << 20),
        name="store",
    )(z, e, m)
    return new_momentum, new_error, weights


def solution(mesh):
    return jax.shard_map(
        body,
        mesh=mesh,
        in_specs=(
            P("replica", None, "fsdp"),
            P(None, "fsdp"),
            P("replica", None, "fsdp"),
            P(None, "fsdp"),
            P("fsdp", None, None),
        ),
        out_specs=(P(None, "fsdp"), P("replica", None, "fsdp"), P()),
        check_vma=False,
    )
```

time: 869 us -> 92.8 us (0.11)
  waiting for transfers between devices: 633 us -> 0 us
  local copies, waits for them, and re-layouts: 176 us -> 0 us
  Pallas kernels: 0 us -> 92.1 us
  matrix products: 23.5 us -> 0 us
  other arithmetic: 20.6 us -> 0 us
  between operations: 14.2 us -> 0.64 us
    all_gather x1 -> x0, waiting for transfers between devices: 445 us -> none  [body(): weights = lax.all_gather(shard_weights, 'fsdp', axis=1, tiled=True)]
    psum x1 -> x0, waiting for transfers between devices: 188 us -> none  [body(): lax.psum(kept_blocks.astype(jnp.bfloat16), 'replica').astype(jnp.float32)]
    gather x2 -> x0, local copies, waits for them, and re-layouts: 99.3 us -> none  [pack_blocks(): return jnp.take_along_axis(flat, positions, axis=2)]
    pallas_call x0 -> x2, Pallas kernels: none -> 92.1 us  [the longest x1 82.8 us: body(): pl.pallas_call(kernel, out_shape=(pltpu.VMEM((rows, shards * cols), BF16)...]
    unnamed x10 -> x0, local copies, waits for them, and re-layouts: 61 us -> none
    dot_general x6 -> x0, matrix products: 23.5 us -> none  [the longest x2 8.14 us: decode(): jnp.einsum('ua,iujb->iajb', cosine_table, halfway, precision=lax.Precisio...]
    transpose x3 -> x0, local copies, waits for them, and re-layouts: 9.41 us -> none  [the longest x2 7.23 us: decode(): jnp.einsum('ua,iujb->iajb', cosine_table, halfway, precision=lax.Precisio...]
  transfers between devices with their start and end apart: 2 -> 0, of which waited for: 2 -> 0; matrix products, arithmetic and copies ran while one was open for 2% -> 0% of each run, Pallas kernels for 0% -> 0%
where the time goes in v1:
time: 92.8 us; the launch traced here: 92.7 us
  Pallas kernels  92.1 us (99%)
    pallas_call x1, Pallas kernels, body(): pl.pallas_call(kernel, out_shape=(pltpu.VMEM((rows, shards * cols), BF16)...  82.8 us
    pallas_call x1, Pallas kernels, body(): pl.pallas_call(store, out_shape=(jax.ShapeDtypeStruct((rows, shards * col...  9.23 us

profile of v1, /device:TPU:1, one launch (start us, length us, event | category | flops | bytes accessed | tf_op | source)
XLA Modules:
  0.0 92.7 jit_solution(12148465920386104879)
XLA Ops:
  0.6 82.8 %step.1 = (bf16[384,28672]{1,0:T(8,128)(2,1)S(1)}, f32[384,1792]{1,0:T(8,128)S(1)}, f32[384,1792]{1,0:T(8,128)S(1)}) custom-call(f32[1,384,1792]{2,1,0:T(8,128)} %local_hbm.1, f32[384,1792]{1,0:T(8,128)} %base_hbm.1, f32[1,384,1792]{2,1,0:T(8,128)} %err_hbm.1, f32[384,1792]{1,0:T(8,128)} %mom_hbm.1, s32[3,14,256]{2,1,0:T(8,128)} %bitcast.1, ...), custom_call_target="tpu_custom_call" | custom-call | tf_op jit(solution)/shard_map/step/pallas_call | solution.py:386
  83.5 9.2 %store.1 = (bf16[384,28672]{1,0:T(8,128)(2,1)}, f32[1,384,1792]{2,1,0:T(8,128)}, f32[384,1792]{1,0:T(8,128)}) custom-call(bf16[384,28672]{1,0:T(8,128)(2,1)S(1)} %get-tuple-element.9.z_ref, f32[384,1792]{1,0:T(8,128)S(1)} %get-tuple-element.10.e_ref, f32[384,1792]{1,0:T(8,128)S(1)} %get-tuple-element.11.m_ref), custom_call_target="tpu_custom_call" | custom-call | tf_op jit(solution)/shard_map/store/pallas_call | solution.py:426

commit v2 on v0

v2 whole, which is shorter than its diff:
```python
import functools

import jax
import jax.numpy as jnp
import ml_dtypes
import numpy as np
from jax import lax
from jax.experimental import pallas as pl
from jax.experimental.pallas import tpu as pltpu
from jax.sharding import PartitionSpec as P

MESH = pl.DeviceIdType.MESH
BLOCK = 128
LOWF = 32
N_REPLICA = 16
F32 = jnp.float32
BF16 = jnp.bfloat16
outer_rate = 0.7
outer_momentum = 0.9
OLD = outer_rate * outer_momentum * outer_momentum
NEW = outer_rate * (1.0 + outer_momentum)

TILES = ((0, 512), (512, 512), (1024, 512), (1536, 256))
STAGES = ((0, 128, 48, 32), (256, 64, 16, 32))
EARLY = 2

WAYS = ("y+", "y-", "z+", "z-", "x+", "x-", "pair")
PLACES = [(a, b) for a in (0, 1, 3, 2) for b in (0, 1, 3, 2)][1:]


def lands(part, a, b, way):
    if way in ("x+", "x-"):
        return "q", a, b
    step = -1 if way[1] == "+" else 1
    if way[0] == "A":
        return part, (a + step) % 4, b
    return part, a, (b + step) % 4


def tasks(stages, k_stage=True, pair="split"):
    todo = []

    def add(name, waits, sends, after=()):
        todo.append((name, tuple(waits), tuple(sends), tuple(after)))

    for s, (_, _, outer, middle) in enumerate(stages):
        parts = [p for p, n in (("m", middle), ("o", outer)) if n]

        def u(p, a, b, h=None):
            return s, p, a % 4, b % 4, h

        own = [(u(p, 0, 0), w + sign) for w in "AB" for p in parts for sign in "+-"]
        add(("own", s), [], own, [("ready", s)])
        for p in parts:

            def x(a, b, way, h=None):
                return [(u(p, a, b, h), way)] if p == "o" else []

            for a, sign, h in ((3, "+", 0), (1, "-", 1)):
                sends = [(u(p, a, 0, h), "A" + sign), (u(p, a, 0), "B+"), (u(p, a, 0), "B-")]
                add(("A", s, p, a), [u(p, a, 0)], sends + x(a, 0, "x" + sign))
                add(("H", s, p, h), [u(p, 2, 0, h)], x(2, 0, "x" + sign, h))
            add(("D", s, p), [], [(u(p, 2, 0), "B+"), (u(p, 2, 0), "B-")], [("H", s, p, 0), ("H", s, p, 1)])
            for a in range(4):
                for b, sign in ((3, "+"), (1, "-")):
                    on = [(u(p, a, b), "B" + sign)] if sign == ("+" if a in (0, 1) else "-") else []
                    add(("B", s, p, a, b), [u(p, a, b)], on + x(a, b, "x" + sign))
                add(("B", s, p, a, 2), [u(p, a, 2)], x(a, 2, "x+" if a in (0, 1) else "x-"))
        for dy, dz in PLACES:
            done = []
            for p in parts:
                a, b = (dy, dz) if p == "m" else (dz, dy)
                done.append(("D", s, p) if (a, b) == (2, 0) else ("A", s, p, a) if b == 0 else ("B", s, p, a, b))
            hs = (0, 1) if (dz, dy) == (2, 0) else (None,)
            waits = [u("q", dz, dy, h) for h in hs] if outer else []
            if pair == "all" or not outer:
                add(("P", s, dy, dz), waits, [(u("all", dy, dz), "pair")], done)
            else:
                add(("PM", s, dy, dz), [], [(u("mo", dy, dz), "pair")], done)
                add(("PQ", s, dy, dz), waits, [(u("q", dz, dy), "pair")])
    if k_stage:
        def u(a, b):
            return 0, "k", a % 4, b % 4, None

        add(("own", "k"), [], [(u(0, 0), w + sign) for w in "AB" for sign in "+-"], [("ready", "k")])
        names = []
        for a, sends in ((3, [(u(3, 0), "A+")]), (1, []), (2, [])):
            add(("A", "k", a), [u(a, 0)], sends + [(u(a, 0), "B+"), (u(a, 0), "B-")])
            names.append(("A", "k", a))
        for a in range(4):
            for b, sign in ((3, "+"), (1, "-")):
                on = [(u(a, b), "B" + sign)] if sign == ("+" if a in (0, 1) else "-") else []
                add(("B", "k", a, b), [u(a, b)], on)
            add(("B", "k", a, 2), [u(a, 2)], [])
            names += [("B", "k", a, b) for b in (1, 2, 3)]
        add(("P", "k"), [], [((0, "k", "all", 0, None), "pair")], names)
    return todo


def rows_of(stages, unit):
    s, p, _, _, h = unit
    _, count, outer, middle = stages[s]
    n = {"m": middle, "o": outer, "q": outer, "all": count, "mo": outer + middle, "k": LOWF * 512 / 1792}[p]
    if p == "k" and unit[2] == "all":
        n *= 16
    return n * (1 if h is None else 0.5)


def order(stages, chain, k_stage=True, pair="split", cs=0.09, cw=0.05, lat=1.0, rate=45.5e3, prate=500e3, t0=0.0):
    todo = tasks(stages, k_stage, pair)
    for n, (name, cost, gap) in enumerate(chain):
        todo.append((name, (), (), (chain[n - 1][0],) if n else ()))
    cost = {name: (c, gap) for name, c, gap in chain}
    rank = {"own": 0, "A": 1, "H": 1, "D": 1, "B": 2, "PM": 4, "PQ": 4, "P": 4}
    arrival, free, done, t, out, left = {}, {}, {}, t0, [], list(todo)
    while left:
        best = None
        for n, (name, waits, sends, after) in enumerate(left):
            if any(k not in done for k in after) or any(k not in arrival for k in waits):
                continue
            ready = max([done[k] for k in after] + [arrival[k] for k in waits] + [0])
            r = 3 if name in cost else rank[name[0]]
            if r == 2 and not sends: r = 4
            key = (max(ready, t), r, ready, n)
            if best is None or key < best[0]:
                best = (key, n)
        key, n = best
        name, waits, sends, after = left.pop(n)
        t = max(t, key[0])
        gap = 0
        if name in cost:
            t += cost[name][0]
            gap = cost[name][1]
        t += cw * len(waits)
        for unit, way in sends:
            t += cs
            s, p, a, b, h = unit
            lane = way
            if way[0] in "AB":
                first = p in ("m", "k")
                lane = ("y" if (way[0] == "A") == first else "z") + way[1]
            size = rows_of(stages, unit) * 1792 * 2
            start = max(t, free.get(lane, 0))
            free[lane] = start + size / (prate if way == "pair" else rate)
            if way == "pair":
                arrival["pair", s] = max(arrival.get(("pair", s), 0), free[lane] + lat)
            else:
                q, a2, b2 = lands(p, a, b, way)
                arrival[s, q, a2, b2, h] = free[lane] + lat
        done[name] = t + gap
        out.append((name, waits, sends))
    return out


def split(values):
    high = values.astype(ml_dtypes.bfloat16)
    low = (values - high.astype(np.float64)).astype(ml_dtypes.bfloat16)
    return high, low


def tables():
    u = np.arange(LOWF, dtype=np.float64)[:, None]
    a = np.arange(BLOCK, dtype=np.float64)[None, :]
    norm = np.where(u == 0, np.sqrt(1.0 / BLOCK), np.sqrt(2.0 / BLOCK))
    low = norm * np.cos(np.pi * (2 * a + 1) * u / (2 * BLOCK))
    diag = np.kron(np.eye(4), low)
    wide = np.concatenate(split(diag), axis=0)
    wide = np.concatenate([wide[:, BLOCK * n : BLOCK * n + BLOCK] for n in range(4)], axis=0)
    high, rest = split(low.T)
    turned = np.concatenate([high, rest, high, np.zeros_like(high)], axis=1)
    narrow = np.concatenate(split(diag.T) + split(low) + (turned,), axis=0)
    return wide, narrow


def mm(a, b):
    return jnp.dot(a, b, preferred_element_type=F32)


def halves(v):
    high = v.astype(BF16)
    return high, (v - high.astype(F32)).astype(BF16)


def three(a, b):
    return mm(a[0], b[0]) + (mm(a[1], b[0]) + mm(a[0], b[1]))


def diagonal(wide, width):
    return jnp.concatenate([wide[256 * n : 256 * n + 256] for n in range(width // BLOCK)], axis=1)


def columns_back(coef, diag):
    return mm(jnp.concatenate([coef, coef], axis=1), diag)


def rows_back(turned, spread):
    high, rest = halves(spread)
    return mm(turned, jnp.concatenate([high, high, rest], axis=0))


def kernel(
    local_hbm, base_hbm, err_hbm, mom_hbm, keep_hbm, wide_hbm, narrow_hbm,
    z_ref, e_ref, m_ref, coef_ref,
    local, base, err, mom, keep, wide, narrow,
    mask, kept, rs_send, rs_recv, part, mean,
    load_sem, red_send, red_recv, out_sem, in_sem,
):
    r, f = lax.axis_index("replica"), lax.axis_index("fsdp")
    x, zh, c = r // 4, (r // 2) % 2, r % 2
    y, zl = f // 4, f % 4
    z = zh * 4 + zl
    cols = e_ref.shape[1]
    group = x * 2 + c
    odd = x % 2

    def at(x_, y_, z_, c_):
        return ((x_ * 2 + z_ // 4) * 2 + c_, y_ * 4 + z_ % 4)

    device = {
        "x+": at((x + 1) % 4, y, z, c), "x-": at((x + 3) % 4, y, z, c),
        "y+": at(x, (y + 1) % 4, z, c), "y-": at(x, (y + 3) % 4, z, c),
        "z+": at(x, y, (z + 1) % 8, c), "z-": at(x, y, (z + 7) % 8, c),
        "far": at(x, y, (z + 4) % 8, c), "pair": at(x, y, z, 1 - c),
    }
    for sign in "+-":
        one, two = device["y" + sign], device["z" + sign]
        device["k", "A" + sign] = tuple(p * (1 - c) + q * c for p, q in zip(one, two, strict=True))
        device["k", "B" + sign] = tuple(p * c + q * (1 - c) for p, q in zip(one, two, strict=True))
    peers = [(group + k) % 8 for k in range(1, 8)]
    peer_device = [at(p // 2, y, z, p % 2) for p in peers]

    loads = {}

    def load(name, src, dst):
        loads[name] = pltpu.make_async_copy(src, dst, load_sem.at[len(loads)])
        loads[name].start()

    blocks = [pl.ds(BLOCK * i, BLOCK) for i in range(3)]
    for i in range(EARLY):
        load(("base", i), base_hbm.at[blocks[i]], base.at[blocks[i]])
        load(("mom", i), mom_hbm.at[blocks[i]], mom.at[blocks[i]])
    load("keep", keep_hbm, keep)
    load("narrow", narrow_hbm, narrow)
    for i in range(3):
        load(("local", i), local_hbm.at[0, blocks[i]], local.at[blocks[i]])
        load(("err", i), err_hbm.at[0, blocks[i]], err.at[blocks[i]])
        if i >= EARLY:
            load(("base", i), base_hbm.at[blocks[i]], base.at[blocks[i]])
    load("wide", wide_hbm, wide)
    for i in range(EARLY, 3):
        load(("mom", i), mom_hbm.at[blocks[i]], mom.at[blocks[i]])

    barrier = pltpu.get_barrier_semaphore()
    partners = [device[k] for k in ("y+", "y-", "z+", "z-", "far")] + peer_device
    for d in partners:
        pl.semaphore_signal(barrier, inc=1, device_id=d, device_id_type=MESH)
    own = pl.multiple_of(f * cols, BLOCK)

    def own_columns(t):
        first, width = TILES[t]
        return pl.ds(pl.multiple_of(own + first, BLOCK), width)

    def without_update():
        for i in range(EARLY):
            loads["base", i].wait()
            loads["mom", i].wait()
            for t, (first, width) in enumerate(TILES):
                span = pl.ds(first, width)
                z_ref[blocks[i], own_columns(t)] = (base[blocks[i], span] - OLD * mom[blocks[i], span]).astype(BF16)
        pl.semaphore_wait(barrier, len(partners))

    def positions(i):
        if i == 0:
            loads["keep"].wait()
        for t, (_, width) in enumerate(TILES):
            at_u, at_v = [], []
            for b in range(width // BLOCK):
                pos = keep[i, pl.ds(4 * t + b, 1), :]
                u = lax.broadcasted_iota(jnp.int32, (LOWF, 256), 0)
                v = lax.broadcasted_iota(jnp.int32, (4 * LOWF, 256), 0)
                at_u.append(jnp.where(u == pos // BLOCK, 1.0, 0.0).astype(BF16))
                at_v.append(jnp.where(v == pos % BLOCK + LOWF * b, 1.0, 0.0).astype(BF16))
            mask[pl.ds(LOWF * i, LOWF), pl.ds(BLOCK * t, BLOCK)] = lax.dot_general(
                jnp.concatenate(at_u, axis=1),
                jnp.concatenate(at_v, axis=1),
                (((1,), (1,)), ((), ())),
                preferred_element_type=F32,
            )

    def encode(i):
        if i == 0:
            loads["narrow"].wait()
        for name in ("base", "local", "err") if i >= EARLY else ("local", "err"):
            loads[name, i].wait()
        low = narrow[1024:1056], narrow[1056:1088]
        for t, (first, width) in enumerate(TILES):
            span = pl.ds(first, width)
            pseudo = base[blocks[i], span] - local[blocks[i], span] + err[blocks[i], span]
            e_ref[blocks[i], span] = pseudo
            half = three(halves(pseudo), (narrow[0:width], narrow[512 : 512 + width]))
            coef = three(low, halves(half))
            place = pl.ds(LOWF * i, LOWF), pl.ds(BLOCK * t, BLOCK)
            kept[place] = coef * mask[place]

    def travel(src, dst, n, device_id):
        copy = pltpu.make_async_remote_copy(
            src_ref=src, dst_ref=dst, send_sem=red_send.at[n], recv_sem=red_recv.at[n],
            device_id=device_id, device_id_type=MESH,
        )
        copy.start()
        return copy

    moving = {}

    def scatter():
        for t in range(4):
            for a in range(2):
                rs_send[4 * a + t] = kept[48 * a : 48 * a + 48, BLOCK * t : BLOCK * t + BLOCK].astype(BF16)
        moving["scatter"] = [travel(rs_send.at[peers[k]], rs_recv.at[k], k, peer_device[k]) for k in range(7)]

    def far():
        total = rs_send[group].astype(F32)
        for k in range(7):
            moving["scatter"][k].wait()
            total = total + rs_recv[k].astype(F32)
        part[0] = total.astype(BF16)
        moving["far"] = travel(part.at[0], part.at[1], 7, device["far"])

    def average():
        moving["far"].wait()
        mean[group] = ((part[0].astype(F32) + part[1].astype(F32)) * (1.0 / N_REPLICA)).astype(BF16)
        moving["mean"] = [travel(mean.at[group], mean.at[group], 8 + k, peer_device[k]) for k in range(7)]

    def averaged():
        for copy in moving["mean"]:
            copy.wait()
        for t in range(4):
            place = pl.ds(BLOCK * t, BLOCK)
            coef_ref[c, f, 0:16, place] = mean[t, pl.ds(pl.multiple_of(c * 32, 16), 16), :]
            coef_ref[c, f, 16:32, place] = mean[t + 4 * c, pl.ds(pl.multiple_of((1 - c) * 16, 16), 16), :]

    def residual(t):
        if t == 0:
            loads["wide"].wait()
        first, width = TILES[t]
        diag, span = diagonal(wide, width), pl.ds(first, width)
        high, rest = halves(kept[:, BLOCK * t : BLOCK * t + BLOCK])
        spread = columns_back(high, diag) + mm(rest, diag[:BLOCK])
        for i in range(3):
            back = rows_back(narrow[1088:1216, : 3 * LOWF], spread[LOWF * i : LOWF * i + LOWF])
            e_ref[blocks[i], span] = e_ref[blocks[i], span] - back

    def step(t):
        if t == 0:
            for i in range(EARLY, 3):
                loads["mom", i].wait()
        first, width = TILES[t]
        diag, span = diagonal(wide, width), pl.ds(first, width)
        spread = columns_back(jnp.concatenate([mean[t], mean[4 + t]], axis=0), diag)
        for i in range(3):
            update = rows_back(narrow[1088:1216, : 3 * LOWF], spread[LOWF * i : LOWF * i + LOWF])
            moved = outer_momentum * mom[blocks[i], span] + update
            m_ref[blocks[i], span] = moved
            if i >= EARLY:
                weights = base[blocks[i], span] - outer_rate * (update + outer_momentum * moved)
                z_ref[blocks[i], own_columns(t)] = weights.astype(BF16)

    nothing = lambda: None
    chain = [(("ready", 0), without_update, 2.6, 0)]
    chain += [(("mask", i), functools.partial(positions, i), 0.8, 0) for i in range(3)]
    chain += [(("encode", i), functools.partial(encode, i), 0.8, 0) for i in range(3)]
    chain += [("scatter", scatter, 0.9, 0)]
    chain += [(("residual", t), functools.partial(residual, t), 0.6, 1.5 * t) for t in (0, 1)]
    chain += [("far", far, 0.8, 0)]
    chain += [(("residual", t), functools.partial(residual, t), 0.6, 3.0 * (t - 2)) for t in (2, 3)]
    chain += [("average", average, 0.9, 2.5), (("ready", "k"), averaged, 0.5, 0)]
    chain += [(("update", t), functools.partial(step, t), 0.7, 0) for t in range(4)]
    chain += [(("ready", 1), nothing, 0, 0)]
    compute = {name: run for name, run, _, _ in chain}

    arrivals, departures, sent, received = {}, {}, {}, {}

    def index(table, key):
        return table.setdefault(key, len(table))

    def copy(unit, way, recv_key):
        s, p, a, b, h = unit
        if p == "k":
            if a == "all":
                ref, rows, width = coef_ref.at[c], 16, 16
            else:
                dy, dz = a + c * (b - a), b + c * (a - b)
                shard = ((y + dy) % 4) * 4 + (zl + dz) % 4
                ref, rows, width = coef_ref.at[c, shard], 16, 1
            target = device["pair"] if way == "pair" else device["k", way]
        else:
            start, count, outer, middle = STAGES[s]
            top = start + c * count
            size = {"m": middle, "o": outer, "q": outer, "mo": outer + middle}
            row = {
                "m": top + outer, "o": top + odd * (outer + middle),
                "q": top + (1 - odd) * (outer + middle), "mo": top + odd * outer,
            }
            dy, dz = (a, b) if p in ("m", "mo") else (b, a)
            column = (((y + dy) % 4) * 4 + (zl + dz) % 4) * cols + (h or 0) * (cols // 2)
            rows, width = size[p], cols if h is None else cols // 2
            ref = z_ref.at[pl.ds(pl.multiple_of(row[p], 16), rows), pl.ds(pl.multiple_of(column, BLOCK), width)]
            axes = {"A": "yz"[p == "o"], "B": "zy"[p == "o"]}
            target = device[axes[way[0]] + way[1] if way[0] in "AB" else way]
        out = s, p, way
        made = pltpu.make_async_remote_copy(
            src_ref=ref, dst_ref=ref, send_sem=out_sem.at[index(departures, out)],
            recv_sem=in_sem.at[index(arrivals, recv_key)], device_id=target, device_id_type=MESH,
        )
        return made, out, rows, width

    def send(unit, way):
        s, p, a, b, h = unit
        key = (s, p, "pair") if way == "pair" else (s,) + lands(p, a, b, way) + (h,)
        made, out, rows, width = copy(unit, way, key)
        sent[out] = (rows, sent.get(out, (rows, 0))[1] + width)
        if way == "pair":
            received[key] = sent[out]
        made.start()

    def arrive(unit):
        copy(unit, "pair", unit)[0].wait_recv()

    for name, waits, sends in order(STAGES, [(n, cost, gap) for n, _, cost, gap in chain]):
        for unit in waits:
            arrive(unit)
        if name in compute:
            compute[name]()
        for unit, way in sends:
            send(unit, way)

    def drain(p, rows, width, out_key, in_key):
        if p == "k":
            ref = coef_ref.at[0, pl.ds(0, width)]
        else:
            ref = z_ref.at[pl.ds(0, rows), pl.ds(0, width)]
        return pltpu.make_async_remote_copy(
            src_ref=ref, dst_ref=ref, send_sem=out_sem.at[departures[out_key]],
            recv_sem=in_sem.at[arrivals[in_key]], device_id=device["pair"], device_id_type=MESH,
        )

    some = next(iter(received))
    for out, (rows, width) in sent.items():
        drain(out[1], rows, width, out, some).wait_send()
    for key, (rows, width) in received.items():
        drain(key[1], rows, width, key, key).wait_recv()


def store(
    z_ref, e_ref, m_ref, coef_ref, wide_hbm, narrow_hbm, w_out, e_out, m_out,
    wide, turned, spread, slots, sem, slot_sem,
):
    cols = e_ref.shape[1]
    tables = [
        pltpu.make_async_copy(wide_hbm, wide, sem.at[10]),
        pltpu.make_async_copy(narrow_hbm.at[pl.ds(1088, BLOCK)], turned, sem.at[11]),
    ]
    copies = [
        pltpu.make_async_copy(
            z_ref.at[pl.ds(EARLY * BLOCK + 16 * k, 16)], w_out.at[pl.ds(EARLY * BLOCK + 16 * k, 16)], sem.at[k]
        )
        for k in range(8)
    ]
    copies.append(pltpu.make_async_copy(e_ref, e_out.at[0], sem.at[8]))
    copies.append(pltpu.make_async_copy(m_ref, m_out, sem.at[9]))
    for copy in tables + copies:
        copy.start()
    for copy in tables:
        copy.wait()
    rows = pl.ds(0, EARLY * BLOCK)
    shards = coef_ref.shape[1]

    def out(slot, shard):
        span = pl.ds(pl.multiple_of(shard * cols, BLOCK), cols)
        return pltpu.make_async_copy(slots.at[slot], w_out.at[rows, span], slot_sem.at[slot])

    for i in range(EARLY):
        for t, (first, width) in enumerate(TILES):
            coef = coef_ref[i, :, :, pl.ds(BLOCK * t, BLOCK)].reshape(shards * LOWF, BLOCK)
            spread[i, :, pl.ds(first, width)] = columns_back(coef, diagonal(wide, width)).astype(BF16)

    table = turned[:, : 2 * LOWF]
    none = jnp.zeros_like(table)
    both = jnp.concatenate(
        [jnp.concatenate([table, none], axis=1), jnp.concatenate([none, table], axis=1)], axis=0
    )

    def place(slot, shard, again):
        if again is not None:
            pl.when(again)(lambda: out(slot, shard).wait())
        lines = pl.ds(pl.multiple_of(shard * LOWF, LOWF), LOWF)
        for first, width in TILES:
            span = pl.ds(first, width)
            one, two = spread[0, lines, span], spread[1, lines, span]
            update = mm(both, jnp.concatenate([one, one, two, two], axis=0))
            before = z_ref[rows, pl.ds(pl.multiple_of(shard * cols + first, BLOCK), width)].astype(F32)
            slots[slot, :, span] = (before - NEW * update).astype(BF16)
        out(slot, shard).start()

    n = slots.shape[0]

    def turn(k, carry):
        for slot in range(n):
            place(slot, k * n + slot, k > 0)
        return carry

    lax.fori_loop(0, shards // n, turn, 0)
    for slot in range(n):
        out(slot, shards - n + slot).wait()
    for copy in copies:
        copy.wait()


def body(local_weights, base_weights, error_buffer, momentum, keep_index):
    rows, cols = base_weights.shape
    shards = lax.axis_size("fsdp")
    wide, narrow = (jnp.asarray(table) for table in tables())
    hbm = pl.BlockSpec(memory_space=pltpu.HBM)
    vmem = pl.BlockSpec(memory_space=pltpu.VMEM)
    z, e, m, coef = pl.pallas_call(
        kernel,
        out_shape=(
            pltpu.VMEM((rows, shards * cols), BF16),
            pltpu.VMEM((rows, cols), F32),
            pltpu.VMEM((rows, cols), F32),
            pltpu.VMEM((EARLY, shards, LOWF, 512), BF16),
        ),
        in_specs=[hbm] * 7,
        out_specs=[vmem] * 4,
        scratch_shapes=[pltpu.VMEM((rows, cols), F32)] * 4
        + [
            pltpu.VMEM((3, 14, 256), jnp.int32),
            pltpu.VMEM((1024, 128), BF16),
            pltpu.VMEM((1216, 128), BF16),
            pltpu.VMEM((96, 512), F32),
            pltpu.VMEM((96, 512), F32),
            pltpu.VMEM((8, 48, 128), BF16),
            pltpu.VMEM((7, 48, 128), BF16),
            pltpu.VMEM((2, 48, 128), BF16),
            pltpu.VMEM((8, 48, 128), BF16),
            pltpu.SemaphoreType.DMA((15,)),
            pltpu.SemaphoreType.DMA((15,)),
            pltpu.SemaphoreType.DMA((15,)),
            pltpu.SemaphoreType.DMA((48,)),
            pltpu.SemaphoreType.DMA((192,)),
        ],
        compiler_params=pltpu.CompilerParams(
            collective_id=1, has_side_effects=True, vmem_limit_bytes=35 << 20
        ),
        name="step",
    )(
        local_weights,
        base_weights,
        error_buffer,
        momentum,
        keep_index.transpose(1, 0, 2),
        wide,
        narrow,
    )
    weights, new_error, new_momentum = pl.pallas_call(
        store,
        out_shape=(
            jax.ShapeDtypeStruct((rows, shards * cols), BF16),
            jax.ShapeDtypeStruct((1, rows, cols), F32),
            jax.ShapeDtypeStruct((rows, cols), F32),
        ),
        in_specs=[vmem] * 4 + [hbm] * 2,
        out_specs=[pl.BlockSpec(memory_space=pl.ANY)] * 3,
        scratch_shapes=[
            pltpu.VMEM((1024, 128), BF16),
            pltpu.VMEM((128, 128), BF16),
            pltpu.VMEM((EARLY, shards * LOWF, cols), BF16),
            pltpu.VMEM((2, EARLY * BLOCK, cols), BF16),
            pltpu.SemaphoreType.DMA((12,)),
            pltpu.SemaphoreType.DMA((2,)),
        ],
        compiler_params=pltpu.CompilerParams(vmem_limit_bytes=6 << 20),
        name="store",
    )(z, e, m, coef, wide, narrow)
    return new_momentum, new_error, weights


def solution(mesh):
    return jax.shard_map(
        body,
        mesh=mesh,
        in_specs=(
            P("replica", None, "fsdp"),
            P(None, "fsdp"),
            P("replica", None, "fsdp"),
            P(None, "fsdp"),
            P("fsdp", None, None),
        ),
        out_specs=(P(None, "fsdp"), P("replica", None, "fsdp"), P()),
        check_vma=False,
    )
```

time: 869 us -> 85.7 us (0.10)
  waiting for transfers between devices: 633 us -> 0 us
  local copies, waits for them, and re-layouts: 176 us -> 0.01 us
  Pallas kernels: 0 us -> 84.9 us
  matrix products: 23.5 us -> 0 us
  other arithmetic: 20.6 us -> 0 us
  between operations: 14.2 us -> 0.67 us
    all_gather x1 -> x0, waiting for transfers between devices: 445 us -> none  [body(): weights = lax.all_gather(shard_weights, 'fsdp', axis=1, tiled=True)]
    psum x1 -> x0, waiting for transfers between devices: 188 us -> none  [body(): lax.psum(kept_blocks.astype(jnp.bfloat16), 'replica').astype(jnp.float32)]
    gather x2 -> x0, local copies, waits for them, and re-layouts: 99.3 us -> none  [pack_blocks(): return jnp.take_along_axis(flat, positions, axis=2)]
    pallas_call x0 -> x2, Pallas kernels: none -> 84.9 us  [the longest x1 70 us: body(): pl.pallas_call(kernel, out_shape=(pltpu.VMEM((rows, shards * cols), BF16)...]
    unnamed x10 -> x4, local copies, waits for them, and re-layouts: 61 us -> 0.01 us
    dot_general x6 -> x0, matrix products: 23.5 us -> none  [the longest x2 8.14 us: decode(): jnp.einsum('ua,iujb->iajb', cosine_table, halfway, precision=lax.Precisio...]
    transpose x3 -> x0, local copies, waits for them, and re-layouts: 9.41 us -> none  [the longest x2 7.23 us: decode(): jnp.einsum('ua,iujb->iajb', cosine_table, halfway, precision=lax.Precisio...]
  transfers between devices with their start and end apart: 2 -> 0, of which waited for: 2 -> 0; matrix products, arithmetic and copies ran while one was open for 2% -> 0% of each run, Pallas kernels for 0% -> 0%
where the time goes in v2:
time: 85.7 us; the launch traced here: 85.6 us
  Pallas kernels  84.9 us (99%)
    pallas_call x1, Pallas kernels, body(): pl.pallas_call(kernel, out_shape=(pltpu.VMEM((rows, shards * cols), BF16)...  70 us
    pallas_call x1, Pallas kernels, body(): pl.pallas_call(store, out_shape=(jax.ShapeDtypeStruct((rows, shards * col...  14.9 us

profile of v2, /device:TPU:1, one launch (start us, length us, event | category | flops | bytes accessed | tf_op | source)
XLA Modules:
  0.0 85.6 jit_solution(11278341224109387396)
XLA Ops:
  0.6 0.0 copy-start
  0.6 0.0 copy-start.1
  0.7 70.0 %step.1 = (bf16[384,28672]{1,0:T(8,128)(2,1)S(1)}, f32[384,1792]{1,0:T(8,128)S(1)}, f32[384,1792]{1,0:T(8,128)S(1)}, bf16[2,16,32,512]{3,2,1,0:T(8,128)(2,1)S(1)}) custom-call(f32[1,384,1792]{2,1,0:T(8,128)} %local_hbm.1, f32[384,1792]{1,0:T(8,128)} %base_hbm.1, f32[1,384,1792]{2,1,0:T(8,128)} %err_hbm.1, f32[384,1792]{1,0:T(8,128)} %mom_hbm.1, ...), custom_call_target="tpu_custom_call" | custom-call | tf_op jit(solution)/shard_map/step/pallas_call | solution.py:525
  70.6 0.0 copy-done
  70.6 0.0 copy-done.1
  70.7 14.9 %store.1 = (bf16[384,28672]{1,0:T(8,128)(2,1)}, f32[1,384,1792]{2,1,0:T(8,128)}, f32[384,1792]{1,0:T(8,128)}) custom-call(bf16[384,28672]{1,0:T(8,128)(2,1)S(1)} %get-tuple-element.10.z_ref, f32[384,1792]{1,0:T(8,128)S(1)} %get-tuple-element.11.e_ref, f32[384,1792]{1,0:T(8,128)S(1)} %get-tuple-element.12.m_ref, ...), custom_call_target="tpu_custom_call" | custom-call | tf_op jit(solution)/shard_map/store/pallas_call | solution.py:565
Async XLA Ops:
  0.6 70.0 %copy-start = (bf16[1216,128]{1,0:T(8,128)(2,1)S(1)}, bf16[1216,128]{1,0:T(8,128)(2,1)}, u32[]{:S(2)}) copy-start(bf16[1216,128]{1,0:T(8,128)(2,1)} %constant.5.clone.narrow_hbm) | copy-start | bytes 933892
  0.6 70.0 %copy-start.1 = (bf16[1024,128]{1,0:T(8,128)(2,1)S(1)}, bf16[1024,128]{1,0:T(8,128)(2,1)}, u32[]{:S(2)}) copy-start(bf16[1024,128]{1,0:T(8,128)(2,1)} %constant.4.clone.wide_hbm) | copy-start | bytes 786436

commit v3 on v2

--- a/solution.py
+++ b/solution.py
@@ -21,7 +21,7 @@
 NEW = outer_rate * (1.0 + outer_momentum)
 
 TILES = ((0, 512), (512, 512), (1024, 512), (1536, 256))
-STAGES = ((0, 128, 48, 32), (256, 64, 16, 32))
+STAGES = ((0, 128, 48, 32), (256, 48, 16, 16), (352, 16, 0, 16))
 EARLY = 2
 
 WAYS = ("y+", "y-", "z+", "z-", "x+", "x-", "pair")
@@ -106,7 +106,7 @@
     return n * (1 if h is None else 0.5)
 
 
-def order(stages, chain, k_stage=True, pair="split", cs=0.09, cw=0.05, lat=1.0, rate=45.5e3, prate=500e3, t0=0.0):
+def order(stages, chain, k_stage=True, pair="split", cs=0.09, cw=0.05, lat=3.0, rate=45.5e3, prate=500e3, t0=0.0):
     todo = tasks(stages, k_stage, pair)
     for n, (name, cost, gap) in enumerate(chain):
         todo.append((name, (), (), (chain[n - 1][0],) if n else ()))
@@ -163,12 +163,14 @@
     a = np.arange(BLOCK, dtype=np.float64)[None, :]
     norm = np.where(u == 0, np.sqrt(1.0 / BLOCK), np.sqrt(2.0 / BLOCK))
     low = norm * np.cos(np.pi * (2 * a + 1) * u / (2 * BLOCK))
+    step = split(-NEW * low.T)
     diag = np.kron(np.eye(4), low)
     wide = np.concatenate(split(diag), axis=0)
     wide = np.concatenate([wide[:, BLOCK * n : BLOCK * n + BLOCK] for n in range(4)], axis=0)
     high, rest = split(low.T)
     turned = np.concatenate([high, rest, high, np.zeros_like(high)], axis=1)
-    narrow = np.concatenate(split(diag.T) + split(low) + (turned,), axis=0)
+    step = np.concatenate(step + (np.zeros((BLOCK, 2 * LOWF), ml_dtypes.bfloat16),), axis=1)
+    narrow = np.concatenate(split(diag.T) + split(low) + (turned, step), axis=0)
     return wide, narrow
 
 
@@ -375,7 +377,7 @@
     chain += [(("residual", t), functools.partial(residual, t), 0.6, 3.0 * (t - 2)) for t in (2, 3)]
     chain += [("average", average, 0.9, 2.5), (("ready", "k"), averaged, 0.5, 0)]
     chain += [(("update", t), functools.partial(step, t), 0.7, 0) for t in range(4)]
-    chain += [(("ready", 1), nothing, 0, 0)]
+    chain += [(("ready", 1), nothing, 0, 0), (("ready", 2), nothing, 0, 0)]
     compute = {name: run for name, run, _, _ in chain}
 
     arrivals, departures, sent, received = {}, {}, {}, {}
@@ -396,12 +398,12 @@
         else:
             start, count, outer, middle = STAGES[s]
             top = start + c * count
-            size = {"m": middle, "o": outer, "q": outer, "mo": outer + middle}
+            size = {"m": middle, "o": outer, "q": outer, "mo": outer + middle, "all": count}
             row = {
                 "m": top + outer, "o": top + odd * (outer + middle),
-                "q": top + (1 - odd) * (outer + middle), "mo": top + odd * outer,
+                "q": top + (1 - odd) * (outer + middle), "mo": top + odd * outer, "all": top,
             }
-            dy, dz = (a, b) if p in ("m", "mo") else (b, a)
+            dy, dz = (a, b) if p in ("m", "mo", "all") else (b, a)
             column = (((y + dy) % 4) * 4 + (zl + dz) % 4) * cols + (h or 0) * (cols // 2)
             rows, width = size[p], cols if h is None else cols // 2
             ref = z_ref.at[pl.ds(pl.multiple_of(row[p], 16), rows), pl.ds(pl.multiple_of(column, BLOCK), width)]
@@ -457,23 +459,26 @@
 ):
     cols = e_ref.shape[1]
     tables = [
-        pltpu.make_async_copy(wide_hbm, wide, sem.at[10]),
-        pltpu.make_async_copy(narrow_hbm.at[pl.ds(1088, BLOCK)], turned, sem.at[11]),
+        pltpu.make_async_copy(wide_hbm, wide, sem.at[3, 0]),
+        pltpu.make_async_copy(narrow_hbm.at[pl.ds(1216, BLOCK)], turned, sem.at[3, 1]),
     ]
-    copies = [
-        pltpu.make_async_copy(
-            z_ref.at[pl.ds(EARLY * BLOCK + 16 * k, 16)], w_out.at[pl.ds(EARLY * BLOCK + 16 * k, 16)], sem.at[k]
-        )
-        for k in range(8)
-    ]
-    copies.append(pltpu.make_async_copy(e_ref, e_out.at[0], sem.at[8]))
-    copies.append(pltpu.make_async_copy(m_ref, m_out, sem.at[9]))
-    for copy in tables + copies:
+    shards = coef_ref.shape[1]
+    n = slots.shape[0]
+    turns = shards // n
+
+    def rest(k):
+        pieces = []
+        for m, (src, dst, first) in enumerate(((z_ref, w_out, EARLY * BLOCK), (e_ref, e_out.at[0], 0), (m_ref, m_out, 0))):
+            height = (src.shape[0] - first) // turns
+            lines = pl.ds(pl.multiple_of(first + height * k, 16), height)
+            pieces.append(pltpu.make_async_copy(src.at[lines], dst.at[lines], sem.at[m, k]))
+        return pieces
+
+    for copy in tables:
         copy.start()
     for copy in tables:
         copy.wait()
     rows = pl.ds(0, EARLY * BLOCK)
-    shards = coef_ref.shape[1]
 
     def out(slot, shard):
         span = pl.ds(pl.multiple_of(shard * cols, BLOCK), cols)
@@ -494,26 +499,27 @@
         if again is not None:
             pl.when(again)(lambda: out(slot, shard).wait())
         lines = pl.ds(pl.multiple_of(shard * LOWF, LOWF), LOWF)
-        for first, width in TILES:
-            span = pl.ds(first, width)
+        for first in range(0, cols, 256):
+            span = pl.ds(first, 256)
             one, two = spread[0, lines, span], spread[1, lines, span]
             update = mm(both, jnp.concatenate([one, one, two, two], axis=0))
-            before = z_ref[rows, pl.ds(pl.multiple_of(shard * cols + first, BLOCK), width)].astype(F32)
-            slots[slot, :, span] = (before - NEW * update).astype(BF16)
+            before = z_ref[rows, pl.ds(pl.multiple_of(shard * cols + first, BLOCK), 256)].astype(F32)
+            slots[slot, :, span] = (before + update).astype(BF16)
         out(slot, shard).start()
 
-    n = slots.shape[0]
-
     def turn(k, carry):
+        for copy in rest(k):
+            copy.start()
         for slot in range(n):
             place(slot, k * n + slot, k > 0)
         return carry
 
-    lax.fori_loop(0, shards // n, turn, 0)
+    lax.fori_loop(0, turns, turn, 0)
     for slot in range(n):
         out(slot, shards - n + slot).wait()
-    for copy in copies:
-        copy.wait()
+    for k in range(turns):
+        for copy in rest(k):
+            copy.wait()
 
 
 def body(local_weights, base_weights, error_buffer, momentum, keep_index):
@@ -536,7 +542,7 @@
         + [
             pltpu.VMEM((3, 14, 256), jnp.int32),
             pltpu.VMEM((1024, 128), BF16),
-            pltpu.VMEM((1216, 128), BF16),
+            pltpu.VMEM((1344, 128), BF16),
             pltpu.VMEM((96, 512), F32),
             pltpu.VMEM((96, 512), F32),
             pltpu.VMEM((8, 48, 128), BF16),
@@ -576,7 +582,7 @@
             pltpu.VMEM((128, 128), BF16),
             pltpu.VMEM((EARLY, shards * LOWF, cols), BF16),
             pltpu.VMEM((2, EARLY * BLOCK, cols), BF16),
-            pltpu.SemaphoreType.DMA((12,)),
+            pltpu.SemaphoreType.DMA((4, 8)),
             pltpu.SemaphoreType.DMA((2,)),
         ],
         compiler_params=pltpu.CompilerParams(vmem_limit_bytes=6 << 20),

time: 85.7 us -> 76.2 us (0.89)
  Pallas kernels: 84.9 us -> 75.5 us
    pallas_call x1, Pallas kernels: 70 us -> 62.7 us  [body(): pl.pallas_call(kernel, out_shape=(pltpu.VMEM((rows, shards * cols), BF16)...]
    pallas_call x1, Pallas kernels: 14.9 us -> 12.8 us  [body(): pl.pallas_call(store, out_shape=(jax.ShapeDtypeStruct((rows, shards * col...]
where the time goes in v3:
time: 76.2 us
  Pallas kernels  75.5 us (99%)
    pallas_call x1, Pallas kernels, body(): pl.pallas_call(kernel, out_shape=(pltpu.VMEM((rows, shards * cols), BF16)...  62.7 us
    pallas_call x1, Pallas kernels, body(): pl.pallas_call(store, out_shape=(jax.ShapeDtypeStruct((rows, shards * col...  12.8 us

profile of v3, /device:TPU:1, one launch (start us, length us, event | category | flops | bytes accessed | tf_op | source)
XLA Modules:
  0.0 76.2 jit_solution(16328354563985600311)
XLA Ops:
  0.6 0.0 copy-start
  0.6 0.0 copy-start.1
  0.7 62.7 %step.1 = (bf16[384,28672]{1,0:T(8,128)(2,1)S(1)}, f32[384,1792]{1,0:T(8,128)S(1)}, f32[384,1792]{1,0:T(8,128)S(1)}, bf16[2,16,32,512]{3,2,1,0:T(8,128)(2,1)S(1)}) custom-call(f32[1,384,1792]{2,1,0:T(8,128)} %local_hbm.1, f32[384,1792]{1,0:T(8,128)} %base_hbm.1, f32[1,384,1792]{2,1,0:T(8,128)} %err_hbm.1, f32[384,1792]{1,0:T(8,128)} %mom_hbm.1, ...), custom_call_target="tpu_custom_call" | custom-call | tf_op jit(solution)/shard_map/step/pallas_call | solution.py:531
  63.3 0.0 copy-done
  63.3 0.0 copy-done.1
  63.4 12.8 %store.1 = (bf16[384,28672]{1,0:T(8,128)(2,1)}, f32[1,384,1792]{2,1,0:T(8,128)}, f32[384,1792]{1,0:T(8,128)}) custom-call(bf16[384,28672]{1,0:T(8,128)(2,1)S(1)} %get-tuple-element.10.z_ref, f32[384,1792]{1,0:T(8,128)S(1)} %get-tuple-element.11.e_ref, f32[384,1792]{1,0:T(8,128)S(1)} %get-tuple-element.12.m_ref, ...), custom_call_target="tpu_custom_call" | custom-call | tf_op jit(solution)/shard_map/store/pallas_call | solution.py:571
Async XLA Ops:
  0.6 62.7 %copy-start = (bf16[1344,128]{1,0:T(8,128)(2,1)S(1)}, bf16[1344,128]{1,0:T(8,128)(2,1)}, u32[]{:S(2)}) copy-start(bf16[1344,128]{1,0:T(8,128)(2,1)} %constant.5.clone.narrow_hbm) | copy-start | bytes 1032196
  0.6 62.7 %copy-start.1 = (bf16[1024,128]{1,0:T(8,128)(2,1)S(1)}, bf16[1024,128]{1,0:T(8,128)(2,1)}, u32[]{:S(2)}) copy-start(bf16[1024,128]{1,0:T(8,128)(2,1)} %constant.4.clone.wide_hbm) | copy-start | bytes 786436

commit v4 on v3

--- a/solution.py
+++ b/solution.py
@@ -476,13 +476,17 @@
 
     for copy in tables:
         copy.start()
+    ahead = turns // 2
+    for k in range(ahead):
+        for copy in rest(k):
+            copy.start()
     for copy in tables:
         copy.wait()
-    rows = pl.ds(0, EARLY * BLOCK)
-
-    def out(slot, shard):
+
+    def out(slot, shard, i):
+        block = pl.ds(BLOCK * i, BLOCK)
         span = pl.ds(pl.multiple_of(shard * cols, BLOCK), cols)
-        return pltpu.make_async_copy(slots.at[slot], w_out.at[rows, span], slot_sem.at[slot])
+        return pltpu.make_async_copy(slots.at[slot, block], w_out.at[block, span], slot_sem.at[slot, i])
 
     for i in range(EARLY):
         for t, (first, width) in enumerate(TILES):
@@ -490,33 +494,35 @@
             spread[i, :, pl.ds(first, width)] = columns_back(coef, diagonal(wide, width)).astype(BF16)
 
     table = turned[:, : 2 * LOWF]
-    none = jnp.zeros_like(table)
-    both = jnp.concatenate(
-        [jnp.concatenate([table, none], axis=1), jnp.concatenate([none, table], axis=1)], axis=0
-    )
 
     def place(slot, shard, again):
-        if again is not None:
-            pl.when(again)(lambda: out(slot, shard).wait())
         lines = pl.ds(pl.multiple_of(shard * LOWF, LOWF), LOWF)
-        for first in range(0, cols, 256):
-            span = pl.ds(first, 256)
-            one, two = spread[0, lines, span], spread[1, lines, span]
-            update = mm(both, jnp.concatenate([one, one, two, two], axis=0))
-            before = z_ref[rows, pl.ds(pl.multiple_of(shard * cols + first, BLOCK), 256)].astype(F32)
-            slots[slot, :, span] = (before + update).astype(BF16)
-        out(slot, shard).start()
+        for i in range(EARLY):
+            pl.when(again)(lambda i=i: out(slot, shard, i).wait())
+            block = pl.ds(BLOCK * i, BLOCK)
+            for first, width in ((0, cols // 2), (cols // 2, cols // 2)):
+                span = pl.ds(first, width)
+                one = spread[i, lines, span]
+                update = mm(table, jnp.concatenate([one, one], axis=0))
+                before = z_ref[block, pl.ds(pl.multiple_of(shard * cols + first, BLOCK), width)].astype(F32)
+                slots[slot, block, span] = (before + update).astype(BF16)
+            out(slot, shard, i).start()
 
     def turn(k, carry):
-        for copy in rest(k):
-            copy.start()
         for slot in range(n):
             place(slot, k * n + slot, k > 0)
+
+        @pl.when(k + ahead < turns)
+        def _():
+            for copy in rest(k + ahead):
+                copy.start()
+
         return carry
 
     lax.fori_loop(0, turns, turn, 0)
     for slot in range(n):
-        out(slot, shards - n + slot).wait()
+        for i in range(EARLY):
+            out(slot, shards - n + slot, i).wait()
     for k in range(turns):
         for copy in rest(k):
             copy.wait()
@@ -552,8 +558,8 @@
             pltpu.SemaphoreType.DMA((15,)),
             pltpu.SemaphoreType.DMA((15,)),
             pltpu.SemaphoreType.DMA((15,)),
-            pltpu.SemaphoreType.DMA((48,)),
-            pltpu.SemaphoreType.DMA((192,)),
+            pltpu.SemaphoreType.DMA((64,)),
+            pltpu.SemaphoreType.DMA((256,)),
         ],
         compiler_params=pltpu.CompilerParams(
             collective_id=1, has_side_effects=True, vmem_limit_bytes=35 << 20
@@ -583,7 +589,7 @@
             pltpu.VMEM((EARLY, shards * LOWF, cols), BF16),
             pltpu.VMEM((2, EARLY * BLOCK, cols), BF16),
             pltpu.SemaphoreType.DMA((4, 8)),
-            pltpu.SemaphoreType.DMA((2,)),
+            pltpu.SemaphoreType.DMA((2, EARLY)),
         ],
         compiler_params=pltpu.CompilerParams(vmem_limit_bytes=6 << 20),
         name="store",

time: 76.2 us -> 76.1 us (level)
    pallas_call x1, Pallas kernels: 12.8 us -> 12 us  [body(): pl.pallas_call(store, out_shape=(jax.ShapeDtypeStruct((rows, shards * col...]
where the time goes in v4:
time: 76.1 us
  Pallas kernels  75.4 us (99%)
    pallas_call x1, Pallas kernels, body(): pl.pallas_call(kernel, out_shape=(pltpu.VMEM((rows, shards * cols), BF16)...  63.4 us
    pallas_call x1, Pallas kernels, body(): pl.pallas_call(store, out_shape=(jax.ShapeDtypeStruct((rows, shards * col...  12 us

profile of v4, /device:TPU:1, one launch (start us, length us, event | category | flops | bytes accessed | tf_op | source)
XLA Modules:
  0.0 76.1 jit_solution(3149926110015411951)
XLA Ops:
  0.6 0.0 copy-start
  0.6 0.0 copy-start.1
  0.7 63.4 %step.1 = (bf16[384,28672]{1,0:T(8,128)(2,1)S(1)}, f32[384,1792]{1,0:T(8,128)S(1)}, f32[384,1792]{1,0:T(8,128)S(1)}, bf16[2,16,32,512]{3,2,1,0:T(8,128)(2,1)S(1)}) custom-call(f32[1,384,1792]{2,1,0:T(8,128)} %local_hbm.1, f32[384,1792]{1,0:T(8,128)} %base_hbm.1, f32[1,384,1792]{2,1,0:T(8,128)} %err_hbm.1, f32[384,1792]{1,0:T(8,128)} %mom_hbm.1, ...), custom_call_target="tpu_custom_call" | custom-call | tf_op jit(solution)/shard_map/step/pallas_call | solution.py:537
  64.0 0.0 copy-done
  64.1 0.0 copy-done.1
  64.1 12.0 %store.1 = (bf16[384,28672]{1,0:T(8,128)(2,1)}, f32[1,384,1792]{2,1,0:T(8,128)}, f32[384,1792]{1,0:T(8,128)}) custom-call(bf16[384,28672]{1,0:T(8,128)(2,1)S(1)} %get-tuple-element.10.z_ref, f32[384,1792]{1,0:T(8,128)S(1)} %get-tuple-element.11.e_ref, f32[384,1792]{1,0:T(8,128)S(1)} %get-tuple-element.12.m_ref, ...), custom_call_target="tpu_custom_call" | custom-call | tf_op jit(solution)/shard_map/store/pallas_call | solution.py:577
Async XLA Ops:
  0.6 63.4 %copy-start = (bf16[1344,128]{1,0:T(8,128)(2,1)S(1)}, bf16[1344,128]{1,0:T(8,128)(2,1)}, u32[]{:S(2)}) copy-start(bf16[1344,128]{1,0:T(8,128)(2,1)} %constant.5.clone.narrow_hbm) | copy-start | bytes 1032196
  0.6 63.4 %copy-start.1 = (bf16[1024,128]{1,0:T(8,128)(2,1)S(1)}, bf16[1024,128]{1,0:T(8,128)(2,1)}, u32[]{:S(2)}) copy-start(bf16[1024,128]{1,0:T(8,128)(2,1)} %constant.4.clone.wide_hbm) | copy-start | bytes 786436

commit v5 on v4

--- a/solution.py
+++ b/solution.py
@@ -106,7 +106,7 @@
     return n * (1 if h is None else 0.5)
 
 
-def order(stages, chain, k_stage=True, pair="split", cs=0.09, cw=0.05, lat=3.0, rate=45.5e3, prate=500e3, t0=0.0):
+def order(stages, chain, k_stage=True, pair="split", cs=0.12, cw=0.06, lat=3.0, rate=45.5e3, prate=500e3, t0=0.0):
     todo = tasks(stages, k_stage, pair)
     for n, (name, cost, gap) in enumerate(chain):
         todo.append((name, (), (), (chain[n - 1][0],) if n else ()))

time: 76.1 us -> 77.5 us (1.018)
  Pallas kernels: 75.4 us -> 76.7 us
    pallas_call x1, Pallas kernels: 63.4 us -> 64.7 us  [body(): pl.pallas_call(kernel, out_shape=(pltpu.VMEM((rows, shards * cols), BF16)...]
where the time goes in v5:
time: 77.5 us; the launch traced here: 77.4 us
  Pallas kernels  76.7 us (99%)
    pallas_call x1, Pallas kernels, body(): pl.pallas_call(kernel, out_shape=(pltpu.VMEM((rows, shards * cols), BF16)...  64.7 us
    pallas_call x1, Pallas kernels, body(): pl.pallas_call(store, out_shape=(jax.ShapeDtypeStruct((rows, shards * col...  12 us

profile of v5, /device:TPU:1, one launch (start us, length us, event | category | flops | bytes accessed | tf_op | source)
XLA Modules:
  0.0 77.4 jit_solution(8092381051169316307)
XLA Ops:
  0.6 0.0 copy-start
  0.6 0.0 copy-start.1
  0.7 64.7 %step.1 = (bf16[384,28672]{1,0:T(8,128)(2,1)S(1)}, f32[384,1792]{1,0:T(8,128)S(1)}, f32[384,1792]{1,0:T(8,128)S(1)}, bf16[2,16,32,512]{3,2,1,0:T(8,128)(2,1)S(1)}) custom-call(f32[1,384,1792]{2,1,0:T(8,128)} %local_hbm.1, f32[384,1792]{1,0:T(8,128)} %base_hbm.1, f32[1,384,1792]{2,1,0:T(8,128)} %err_hbm.1, f32[384,1792]{1,0:T(8,128)} %mom_hbm.1, ...), custom_call_target="tpu_custom_call" | custom-call | tf_op jit(solution)/shard_map/step/pallas_call | solution.py:537
  65.4 0.0 copy-done
  65.4 0.0 copy-done.1
  65.4 12.0 %store.1 = (bf16[384,28672]{1,0:T(8,128)(2,1)}, f32[1,384,1792]{2,1,0:T(8,128)}, f32[384,1792]{1,0:T(8,128)}) custom-call(bf16[384,28672]{1,0:T(8,128)(2,1)S(1)} %get-tuple-element.10.z_ref, f32[384,1792]{1,0:T(8,128)S(1)} %get-tuple-element.11.e_ref, f32[384,1792]{1,0:T(8,128)S(1)} %get-tuple-element.12.m_ref, ...), custom_call_target="tpu_custom_call" | custom-call | tf_op jit(solution)/shard_map/store/pallas_call | solution.py:577
Async XLA Ops:
  0.6 64.8 %copy-start = (bf16[1344,128]{1,0:T(8,128)(2,1)S(1)}, bf16[1344,128]{1,0:T(8,128)(2,1)}, u32[]{:S(2)}) copy-start(bf16[1344,128]{1,0:T(8,128)(2,1)} %constant.5.clone.narrow_hbm) | copy-start | bytes 1032196
  0.6 64.8 %copy-start.1 = (bf16[1024,128]{1,0:T(8,128)(2,1)S(1)}, bf16[1024,128]{1,0:T(8,128)(2,1)}, u32[]{:S(2)}) copy-start(bf16[1024,128]{1,0:T(8,128)(2,1)} %constant.4.clone.wide_hbm) | copy-start | bytes 786436
